TPU v7x, 32 devices: a whole 2x2x4 slice. The times are simulated.
32 devices in a mesh: groups: 2 (over y), freq: 4 (over z), read: 2 (over x), pair: 2 (over core).
Axes of the slice: x: 2, y: 2, z: 4, core: 2. Of those that a mesh axis runs over, the one named last changes fastest.
Arguments:
- exposures: float32 [8, 2048, 2048], P(('groups', 'read', 'pair'), 'freq'), parts along dimension 0, may hold values from -6 to 6
- stamps: float32 [8, 16, 16], P('groups'), parts along dimension 0, may hold values from -1 to 1, as said below
- zero_point: float32 [8], P('groups'), parts along dimension 0, may hold values from 0.5 to 2
- noise_var: float32 [8], P('groups'), parts along dimension 0, may hold values from 0.25 to 4
- footprint: int32 [8, 2], P('groups'), parts along dimension 0, may hold values from 0 to 2048, as said below
- accept: int32 [8], P('groups'), parts along dimension 0, may hold values from 0 to 1, as said below
- assign: int32 [8], P('groups'), parts along dimension 0, may hold values from 0 to 3, each once
Outputs:
- coadd: float32 [2, 4096, 1024], P(None, ('groups', 'read', 'pair'), 'freq'), parts along dimension 1
There are 2 independent parts, one for each index of `groups`. A program takes and returns all parts, laid end to end along the dimension named above; each array names one. Nothing has to cross between parts.
Inputs may be any that keep to these rules, and one draw needn't show every extreme that they name: `stamps`: each stamp is 1 at row 8 and column 8, and the absolute values of its other entries sum to at most 0.9. For every exposure footprint[e, 0] < footprint[e, 1] and the two differ by at least 512; some exposure covers all 2048 rows. `accept`: at least one exposure is rejected, and at least one exposure that covers all 2048 rows is accepted. `assign`: each exposure sits in exactly one slot.
All inputs are finite; a program needn't handle non-finite values.
Results may differ from a plain program's by a relative error of at most 0.0001.
Values sent between devices are 32-bit elements; how exact they have to be, the bound alone decides.
A program may use at most 64 MiB of HBM per device.

v0:
```python
import math
import jax
import jax.numpy as jnp
from jax import lax
from jax.sharding import PartitionSpec as P

HIGHEST = lax.Precision.HIGHEST
TWO_PI = 2.0 * math.pi
LANES = 128


def with_halo(block, sides, width):
    for axis, dim in sides:
        count = lax.axis_size(axis)
        forward = [(i, i + 1) for i in range(count - 1)]
        backward = [(target, source) for source, target in forward]
        low = lax.ppermute(
            lax.slice_in_dim(block, block.shape[dim] - width, None, axis=dim), axis, forward
        )
        high = lax.ppermute(lax.slice_in_dim(block, 0, width, axis=dim), axis, backward)
        block = jnp.concatenate([low, block, high], axis=dim)
    return block


def phase_table(left_ids, right_ids, modulus):
    product = left_ids[:, None] * right_ids[None, :] % modulus
    return product.astype(jnp.float32) * (TWO_PI / modulus)


def fourier(real_in, imag_in, length):
    outer = length // LANES
    lead = real_in.shape[:-1]
    outer_ids = jnp.arange(outer, dtype=jnp.int32)
    lane_ids = jnp.arange(LANES, dtype=jnp.int32)
    short_phase = phase_table(outer_ids, outer_ids, outer)
    cos_a = jnp.cos(short_phase)
    sin_a = jnp.sin(short_phase)
    shaped_re = real_in.reshape(lead + (outer, LANES))
    first_re = jnp.einsum("...ab,ad->...db", shaped_re, cos_a, precision=HIGHEST)
    first_im = -jnp.einsum("...ab,ad->...db", shaped_re, sin_a, precision=HIGHEST)
    if imag_in is not None:
        shaped_im = imag_in.reshape(lead + (outer, LANES))
        first_re = first_re + jnp.einsum("...ab,ad->...db", shaped_im, sin_a, precision=HIGHEST)
        first_im = first_im + jnp.einsum("...ab,ad->...db", shaped_im, cos_a, precision=HIGHEST)
    twist = phase_table(outer_ids, lane_ids, length)
    twist_cos = jnp.cos(twist)
    twist_sin = jnp.sin(twist)
    mid_re = first_re * twist_cos + first_im * twist_sin
    mid_im = first_im * twist_cos - first_re * twist_sin
    lane_phase = phase_table(lane_ids, lane_ids, LANES)
    cos_b = jnp.cos(lane_phase)
    sin_b = jnp.sin(lane_phase)
    out_re = jnp.einsum("...db,bc->...cd", mid_re, cos_b, precision=HIGHEST) + jnp.einsum(
        "...db,bc->...cd", mid_im, sin_b, precision=HIGHEST
    )
    out_im = jnp.einsum("...db,bc->...cd", mid_im, cos_b, precision=HIGHEST) - jnp.einsum(
        "...db,bc->...cd", mid_re, sin_b, precision=HIGHEST
    )
    return (out_re.reshape(lead + (length,)), out_im.reshape(lead + (length,)))


def pack_blocks(real_part, imag_part, blocks):
    lead = real_part.shape[:-1]
    slice_width = real_part.shape[-1] // blocks
    both = jnp.stack(
        [
            real_part.reshape(lead + (blocks, slice_width)),
            imag_part.reshape(lead + (blocks, slice_width)),
        ],
        axis=-2,
    )
    return both.reshape(lead + (blocks * 2 * slice_width,))


def stamp_columns(stamp_set, freq_ids, image_width):
    stamp_len = stamp_set.shape[1]
    offsets = jnp.arange(stamp_len, dtype=jnp.int32) - stamp_len // 2
    phases = phase_table(jnp.mod(offsets, image_width), freq_ids, image_width)
    q_real = jnp.einsum("nab,bp->nap", stamp_set, jnp.cos(phases), precision=HIGHEST)
    q_imag = -jnp.einsum("nab,bp->nap", stamp_set, jnp.sin(phases), precision=HIGHEST)
    return (q_real, q_imag)


def psf_spectrum(stamp_set, rows_u, freq_ids, image_height, image_width):
    stamp_len = stamp_set.shape[1]
    q_real, q_imag = stamp_columns(stamp_set, freq_ids, image_width)
    offsets = jnp.arange(stamp_len, dtype=jnp.int32) - stamp_len // 2
    phases = phase_table(rows_u, jnp.mod(offsets, image_height), image_height)
    cos_u = jnp.cos(phases)
    sin_u = jnp.sin(phases)
    p_real = jnp.einsum("ma,nap->nmp", cos_u, q_real, precision=HIGHEST) + jnp.einsum(
        "ma,nap->nmp", sin_u, q_imag, precision=HIGHEST
    )
    p_imag = jnp.einsum("ma,nap->nmp", cos_u, q_imag, precision=HIGHEST) - jnp.einsum(
        "ma,nap->nmp", sin_u, q_real, precision=HIGHEST
    )
    return (p_real, p_imag)


def per_device(exposures, stamps, zero_point, noise_var, footprint, accept, assign):
    exp_dev, rows_dev, image_width = exposures.shape
    freq_count = lax.axis_size("freq")
    reader_count = lax.axis_size(("read", "pair"))
    image_height = rows_dev * freq_count
    half_width = image_width // 2
    per_freq = half_width // freq_count
    out_rows = image_height // reader_count
    count_all = assign.shape[0]
    freq_at = lax.axis_index("freq")
    reader_at = lax.axis_index(("read", "pair"))
    labels = jnp.arange(count_all, dtype=jnp.int32)
    slot_ids = reader_at * exp_dev + jnp.arange(exp_dev, dtype=jnp.int32)
    owner_id = jnp.sum(jnp.where(slot_ids[:, None] == labels[None, :], assign[None, :], 0), axis=1)
    chosen = owner_id[:, None] == labels[None, :]
    low_row = jnp.sum(jnp.where(chosen, footprint[None, :, 0], 0), axis=1)
    high_row = jnp.sum(jnp.where(chosen, footprint[None, :, 1], 0), axis=1)
    accepted = accept.astype(jnp.float32)
    numer_weight = accepted * zero_point / noise_var
    denom_weight = accepted * zero_point * zero_point / noise_var
    local_weight = jnp.sum(jnp.where(chosen, numer_weight[None, :], 0.0), axis=1)
    local_stamps = jnp.sum(jnp.where(chosen[:, :, None, None], stamps[None], 0.0), axis=1)
    padded = with_halo(exposures, (("freq", 1),), 1)
    zero_col = jnp.zeros((exp_dev, rows_dev, 1), jnp.float32)
    left_cells = jnp.concatenate([zero_col, exposures[:, :, :-1]], axis=2)
    right_cells = jnp.concatenate([exposures[:, :, 1:], zero_col], axis=2)
    row_global = freq_at * rows_dev + jnp.arange(rows_dev, dtype=jnp.int32)
    inside = (row_global[None, :] >= low_row[:, None]) & (row_global[None, :] < high_row[:, None])
    beside = padded[:, :-2] + padded[:, 2:] + left_cells + right_cells
    cleaned = jnp.where(inside[:, :, None], exposures - 0.25 * beside, 0.0)
    rows_out = reader_at * out_rows + jnp.arange(out_rows, dtype=jnp.int32)
    cols_own = freq_at * per_freq + jnp.arange(per_freq, dtype=jnp.int32)
    all_real, all_imag = psf_spectrum(stamps, rows_out, cols_own, image_height, image_width)
    denom = jnp.einsum(
        "n,nmp->mp", denom_weight, all_real * all_real + all_imag * all_imag, precision=HIGHEST
    )
    spec_re, spec_im = fourier(cleaned, None, image_width)
    packed = pack_blocks(spec_re[:, :, :half_width], spec_im[:, :, :half_width], freq_count)
    spectra = jnp.transpose(packed, (1, 0, 2)).reshape(rows_dev, exp_dev, freq_count, 2 * per_freq)
    regrouped = lax.all_to_all(spectra, "freq", split_axis=2, concat_axis=0, tiled=True)
    regrouped = regrouped.reshape(image_height, exp_dev, 2, per_freq)
    col_re = jnp.transpose(regrouped[:, :, 0], (1, 2, 0))
    col_im = jnp.transpose(regrouped[:, :, 1], (1, 2, 0))
    grid_re, grid_im = fourier(col_re, col_im, image_height)
    rows_u = jnp.arange(out_rows * lax.axis_size(("read", "pair")), dtype=jnp.int32)
    kernel_real, kernel_imag = psf_spectrum(
        local_stamps, rows_u, cols_own, image_height, image_width
    )
    term_real = jnp.einsum(
        "e,emp,epm->mp", local_weight, kernel_real, grid_re, precision=HIGHEST
    ) + jnp.einsum("e,emp,epm->mp", local_weight, kernel_imag, grid_im, precision=HIGHEST)
    term_imag = jnp.einsum(
        "e,emp,epm->mp", local_weight, kernel_real, grid_im, precision=HIGHEST
    ) - jnp.einsum("e,emp,epm->mp", local_weight, kernel_imag, grid_re, precision=HIGHEST)
    summed = lax.psum_scatter(
        jnp.concatenate([term_real, term_imag], axis=1),
        ("read", "pair"),
        scatter_dimension=0,
        tiled=True,
    )
    numer_real = summed[:, :per_freq]
    numer_imag = summed[:, per_freq:]
    scale = 1.0 / math.sqrt(image_height * image_width)
    root = jnp.sqrt(denom)
    return jnp.stack([numer_real / root * scale, numer_imag / root * scale])


def solution(mesh):
    in_specs = (
        P(("groups", "read", "pair"), "freq", None),
        P("groups", None, None),
        P("groups"),
        P("groups"),
        P("groups", None),
        P("groups"),
        P("groups"),
    )
    out_specs = P(None, ("groups", "read", "pair"), "freq")
    return jax.shard_map(
        per_device, mesh=mesh, in_specs=in_specs, out_specs=out_specs, check_vma=False
    )
```

profile of v0, /device:TPU:0, one launch (start us, length us, event | category | flops | bytes accessed | tf_op | source)
XLA Modules:
  0.0 307.0 jit_solution(17262272560458219443)
XLA Ops:
  7.4 4.9 %collective-permute-start = (f32[1,1,2048]{2,1,0:T(1,128)S(1)}, f32[1,1,2048]{2,1,0:T(1,128)S(1)}, u32[]{:S(2)}, u32[]{:S(2)}) collective-permute-start(f32[1,1,2048]{2,1,0:T(1,128)S(1)} %get-tuple-element.17), channel_id=1, source_target_pairs={{0,4},{4,8},{8,12},{1,5},{5,9},{9,13},{2,6},{6,10},{10,14},{3,7},{... | collective-permute-start | bytes 24584 | tf_op jit(solution)/shard_map/ppermute | solution.py:17
  13.7 8.0 %fusion.260 = (f32[1,512,2047]{2,1,0:T(8,128)}, f32[1,512,2047]{2,1,0:T(8,128)}) fusion(f32[1,512,2048]{2,1,0:T(8,128)} %param.7), kind=kLoop, calls=%fused_computation.295 | loop fusion | bytes 16769024 | tf_op jit(solution)/shard_map/slice | solution.py:124
  22.4 1.3 fusion.152
  23.7 1.3 fusion.151
  25.1 9.1 %fusion.6 = f32[64,8,16,128]{3,1,2,0:T(8,128)S(1)} fusion(f32[1,512,2048]{2,1,0:T(8,128)} %param.7, f32[1,1,2048]{2,1,0:T(1,128)S(1)} %collective-permute-done.1, f32[1,1,2048]{2,1,0:T(1,128)S(1)} %collective-permute-done, f32[1,512,2047]{2,1,0:T(8,128)} %get-tuple-element.16, f32[1,512,2047]{2,1,0:T(8,128)} %get-tuple-element.15, pred[512]{0:T(512)(128)(4,1)S(1)} %fusion.151), kind=kLoop, calls=%fused_computation.7 | loop fusion | flops 8388608 | bytes 16790016
  35.1 4.0 %fusion.119 = f32[16,512,128]{2,0,1:T(8,128)S(1)} fusion(f32[512,16,128]{2,1,0:T(8,128)S(1)} %bitcast.210), kind=kOutput, calls=%fused_computation.151 | convolution fusion | flops 201330176 | bytes 8388608 | tf_op jit(solution)/shard_map/...ab,ad->...db/dot_general | solution.py:40
  39.1 4.8 %fusion.8 = (f32[512,16,128]{2,1,0:T(8,128)S(1)}, f32[512,16,128]{2,1,0:T(8,128)S(1)}) fusion(f32[16,512,128]{2,0,1:T(8,128)S(1)} %fusion.119, f32[16,128]{1,0:T(8,128)S(1)} %get-tuple-element.23, f32[16,128]{1,0:T(8,128)S(1)} %get-tuple-element.24, f32[512,16,128]{2,1,0:T(8,128)S(1)} %bitcast.211), kind=kOutput, calls=%fused_computation.14 | convolution fusion | flops 208670208 | bytes 16793600 | tf_op jit(solution)/shard_map/...ab,ad->...db/dot_general | solution.py:39
  44.0 5.9 %fusion.13 = f32[128,512,16]{1,0,2:T(8,128)S(1)} fusion(f32[512,16,128]{2,1,0:T(8,128)S(1)} %get-tuple-element.8), kind=kOutput, calls=%fused_computation.23 | convolution fusion | flops 1610842112 | bytes 8388608 | tf_op jit(solution)/shard_map/...db,bc->...cd/dot_general | solution.py:53
  49.9 5.4 %fusion.11 = f32[128,512,16]{1,0,2:T(8,128)S(1)} fusion(f32[512,16,128]{2,1,0:T(8,128)S(1)} %get-tuple-element.8), kind=kOutput, calls=%fused_computation.21 | convolution fusion | flops 1610842112 | bytes 8388608 | tf_op jit(solution)/shard_map/...db,bc->...cd/dot_general | solution.py:56
  55.3 6.2 %add_bitcast_fusion = f32[1,512,128,16]{1,2,3,0:T(8,128)S(1)} fusion(f32[128,512,16]{1,0,2:T(8,128)S(1)} %fusion.13, f32[512,16,128]{2,1,0:T(8,128)S(1)} %get-tuple-element.7), kind=kOutput, calls=%fused_computation.20 | convolution fusion | flops 1611890688 | bytes 12582912 | tf_op jit(solution)/shard_map/...db,bc->...cd/dot_general | solution.py:53
  61.5 2.4 copy.70
  64.1 5.9 %subtract_bitcast_fusion = f32[1,512,128,16]{1,2,3,0:T(8,128)S(1)} fusion(f32[128,512,16]{1,0,2:T(8,128)S(1)} %fusion.11, f32[512,16,128]{2,1,0:T(8,128)S(1)} %get-tuple-element.7), kind=kOutput, calls=%fused_computation.19 | convolution fusion | flops 1611890688 | bytes 12582912 | tf_op jit(solution)/shard_map/...db,bc->...cd/dot_general | solution.py:56
  70.0 2.6 copy.73
  73.3 2.7 copy.74
  76.0 6.1 %all-to-all-start = ((f32[512,1,4,512]{0,3,1,2:T(8,128)}), f32[512,1,4,512]{0,3,1,2:T(8,128)}, u32[]{:S(2)}, u32[]{:S(2)}) async-start(f32[512,1,4,512]{0,3,1,2:T(8,128)} %bitcast.212), calls=%async_computation | async-start | bytes 8388608 | tf_op jit(solution)/shard_map/all_to_all | solution.py:139
  82.9 1.3 multiply_divide_fusion
  84.8 5.7 %fusion.61 = f32[256,2048]{1,0:T(8,128)S(1)} fusion(f32[16,256]{1,0:T(8,128)S(1)} %fusion.129, s32[16]{0:T(128)S(1)} %and_select_fusion), kind=kOutput, calls=%fused_computation.88 | convolution fusion | flops 101122048 | bytes 2113600 | tf_op jit(solution)/shard_map/ma,nap->nmp/dot_general | solution.py:91
  90.5 7.2 %fusion.59 = f32[256,2048]{1,0:T(8,128)} fusion(f32[16,256]{1,0:T(8,128)S(1)} %convolution_negate_fusion.1, s32[16]{0:T(128)S(1)} %and_select_fusion), kind=kOutput, calls=%fused_computation.87 | convolution fusion | flops 101122048 | bytes 2113600 | tf_op jit(solution)/shard_map/ma,nap->nmp/dot_general | solution.py:94
  97.8 7.8 %fusion.22 = f32[2048,256]{0,1:T(8,128)} fusion(f32[256,2048]{1,0:T(8,128)S(1)} %fusion.61, f32[16,256]{1,0:T(8,128)S(1)} %convolution_negate_fusion.1, f32[]{:T(128)} %get-tuple-element.22, s32[16]{0:T(128)S(1)} %and_select_fusion), kind=kOutput, calls=%fused_computation.34 | convolution fusion | flops 102170624 | bytes 4210756 | tf_op jit(solution)/shard_map/ma,nap->nmp/dot_general | solution.py:91
  105.6 69.5 %all-to-all-done = f32[512,1,4,512]{0,3,1,2:T(8,128)} async-done(((f32[512,1,4,512]{0,3,1,2:T(8,128)}), f32[512,1,4,512]{0,3,1,2:T(8,128)}, u32[]{:S(2)}, u32[]{:S(2)}) %all-to-all-start) | async-done | bytes 4194336 | tf_op jit(solution)/shard_map/all_to_all | solution.py:139
  175.0 5.3 %copy.76 = f32[4,512,1,1,512]{4,1,0,3,2:T(8,128)} copy(f32[4,512,1,1,512]{1,4,0,3,2:T(8,128)} %bitcast.25) | data formatting | bytes 8388608 | tf_op jit(solution)/shard_map/all_to_all | solution.py:139
  180.3 5.9 %reshape.291 = f32[2048,1,2,256]{3,2,0,1:T(2,128)} reshape(f32[4,512,1,1,512]{4,1,0,3,2:T(8,128)} %copy.76) | data formatting | bytes 8388608 | tf_op jit(solution)/shard_map/reshape | solution.py:140
  186.2 7.6 %slice_bitcast_fusion = (f32[1,256,2048]{1,0,2:T(1,128)}, f32[1,256,2048]{1,0,2:T(1,128)S(1)}) fusion(f32[2048,1,2,256]{3,2,0,1:T(2,128)} %reshape.291), kind=kLoop, calls=%fused_computation.35 | loop fusion | bytes 8388608 | tf_op jit(solution)/shard_map/transpose | solution.py:142
  193.7 1.5 copy.93
  195.2 2.2 copy.91
  197.5 3.3 %fusion.116 = f32[16,256,128]{2,0,1:T(8,128)} fusion(f32[256,16,128]{2,1,0:T(8,128)S(1)} %copy.91), kind=kOutput, calls=%fused_computation.148 | convolution fusion | flops 100666880 | bytes 4194304 | tf_op jit(solution)/shard_map/...ab,ad->...db/dot_general | solution.py:40
  200.7 3.3 %fusion.122 = f32[16,256,128]{2,0,1:T(8,128)} fusion(f32[256,16,128]{2,1,0:T(8,128)S(1)} %copy.91), kind=kOutput, calls=%fused_computation.154 | convolution fusion | flops 100666880 | bytes 4194304 | tf_op jit(solution)/shard_map/...ab,ad->...db/dot_general | solution.py:39
  204.0 1.4 copy.94
  205.5 2.7 copy.92
  209.5 3.8 %negate_add_fusion = f32[16,256,128]{2,0,1:T(8,128)S(1)} fusion(f32[16,256,128]{2,0,1:T(8,128)} %fusion.116, f32[256,16,128]{2,1,0:T(8,128)S(1)} %copy.92), kind=kOutput, calls=%fused_computation.55 | convolution fusion | flops 101715456 | bytes 6291456 | tf_op jit(solution)/shard_map/...ab,ad->...db/dot_general | solution.py:44
  213.3 4.0 %fusion.31 = (f32[256,16,128]{2,1,0:T(8,128)S(1)}, f32[256,16,128]{2,1,0:T(8,128)S(1)}) fusion(f32[16,256,128]{2,0,1:T(8,128)S(1)} %negate_add_fusion, f32[16,128]{1,0:T(8,128)S(1)} %get-tuple-element.23, f32[16,128]{1,0:T(8,128)S(1)} %get-tuple-element.24, f32[16,256,128]{2,0,1:T(8,128)S(1)} %copy-done.2, f32[256,16,128]{2,1,0:T(8,128)} %copy-done), kind=kOutput, calls=%fused_computation.48 | convolution fusion | flops 104336896 | bytes 10502144 | tf_op jit(solution)/shard_map/...ab,ad->...db/dot_general | solution.py:43
  217.3 2.6 fusion.36
  219.9 3.9 %fusion.34 = f32[128,256,16]{1,0,2:T(8,128)} fusion(f32[256,16,128]{2,1,0:T(8,128)S(1)} %get-tuple-element.12), kind=kOutput, calls=%fused_computation.56 | convolution fusion | flops 805535744 | bytes 4194304 | tf_op jit(solution)/shard_map/...db,bc->...cd/dot_general | solution.py:56
  223.8 2.8 add_bitcast_fusion.1
  226.6 2.5 copy.81
  229.1 2.9 copy.82
  232.0 4.2 %subtract_bitcast_fusion.1 = f32[1,256,128,16]{1,2,3,0:T(8,128)S(1)} fusion(f32[128,256,16]{1,0,2:T(8,128)} %fusion.34, f32[256,16,128]{2,1,0:T(8,128)S(1)} %get-tuple-element.11), kind=kOutput, calls=%fused_computation.53 | convolution fusion | flops 806060032 | bytes 6291456 | tf_op jit(solution)/shard_map/...db,bc->...cd/dot_general | solution.py:56
  236.2 2.5 copy.85
  238.8 3.1 %copy.86 = f32[256,2048]{1,0:T(8,128)} copy(f32[256,2048]{0,1:T(8,128)} %bitcast.218) | data formatting | bytes 4194304 | tf_op jit(solution)/shard_map/reshape.71
  241.9 9.1 %fusion.28 = (f32[2048,256]{0,1:T(8,128)S(1)}, f32[2048,256]{0,1:T(8,128)S(1)}) fusion(f32[256,2048]{1,0:T(8,128)} %copy.86, f32[2048,256]{0,1:T(8,128)} %fusion.22, f32[256,2048]{1,0:T(8,128)S(1)} %copy-done.1, f32[256,2048]{1,0:T(8,128)} %fusion.59, f32[16,256]{1,0:T(8,128)S(1)} %fusion.129, s32[16]{0:T(128)S(1)} %and_select_fusion, f32[]{:T(128)} %get-tuple-element.22), kind=kOutput, calls=%fused_computation.41 | convolution fusion | flops 105316352 | bytes 12599364 | tf_op jit(solution)/shard_map/ma,nap->nmp/dot_general | solution.py:94
  250.9 2.4 pad_maximum_fusion.3
  254.1 2.0 fusion.83
  256.1 1.9 fusion.85
  258.0 2.0 fusion.87
  260.0 2.5 fusion.27
  262.5 34.6 %reduce-scatter.2.cloned.1.call-done = f32[512,512]{0,1:T(8,128)} async-done(((f32[2048,512]{0,1:T(8,128)}), f32[512,512]{0,1:T(8,128)}) %reduce-scatter.2.cloned.1.call-update) | async-done | bytes 1048592 | tf_op jit(solution)/shard_map/reduce_scatter | solution.py:154
  297.1 1.4 fusion.56
  298.6 1.3 copy.87
  (42 shorter events, 8.1 us)
Async XLA Ops:
  7.4 17.6 %collective-permute-start = (f32[1,1,2048]{2,1,0:T(1,128)S(1)}, f32[1,1,2048]{2,1,0:T(1,128)S(1)}, u32[]{:S(2)}, u32[]{:S(2)}) collective-permute-start(f32[1,1,2048]{2,1,0:T(1,128)S(1)} %get-tuple-element.17), channel_id=1, source_target_pairs={{0,4},{4,8},{8,12},{1,5},{5,9},{9,13},{2,6},{6,10},{10,14},{3,7},{... | collective-permute-start | bytes 24584 | tf_op jit(solution)/shard_map/ppermute | solution.py:17
  12.4 12.7 %collective-permute-start.1 = (f32[1,1,2048]{2,1,0:T(1,128)S(1)}, f32[1,1,2048]{2,1,0:T(1,128)S(1)}, u32[]{:S(2)}, u32[]{:S(2)}) collective-permute-start(f32[1,1,2048]{2,1,0:T(1,128)S(1)} %get-tuple-element.18), channel_id=1, source_target_pairs={{4,0},{8,4},{12,8},{5,1},{9,5},{13,9},{6,2},{10,6},{14,10},{7,3},{... | collective-permute-start | bytes 24584 | tf_op jit(solution)/shard_map/ppermute | solution.py:20
  13.7 8.1 %copy-start.9 = (s32[4]{0:T(128)S(1)}, s32[4]{0:T(128)}, u32[]{:S(2)}) copy-start(s32[4]{0:T(128)} %param.13) | copy-start | bytes 52
  13.7 8.7 %copy-start.5 = (s32[4,2]{0,1:T(2,128)S(1)}, s32[4,2]{0,1:T(2,128)}, u32[]{:S(2)}) copy-start(s32[4,2]{0,1:T(2,128)} %param.11) | copy-start | bytes 100
  76.0 6.8 %copy-start.4 = (f32[4,16,16]{2,1,0:T(8,128)S(1)}, f32[4,16,16]{2,1,0:T(8,128)}, u32[]{:S(2)}) copy-start(f32[4,16,16]{2,1,0:T(8,128)} %param.8) | copy-start | bytes 12292
  76.0 6.9 %copy-start.6 = (f32[4]{0:T(128)S(1)}, f32[4]{0:T(128)}, u32[]{:S(2)}) copy-start(f32[4]{0:T(128)} %param.10) | copy-start | bytes 52
  76.0 6.9 %copy-start.7 = (f32[4]{0:T(128)S(1)}, f32[4]{0:T(128)}, u32[]{:S(2)}) copy-start(f32[4]{0:T(128)} %param.9) | copy-start | bytes 52
  76.0 6.9 %copy-start.8 = (s32[4]{0:T(128)S(1)}, s32[4]{0:T(128)}, u32[]{:S(2)}) copy-start(s32[4]{0:T(128)} %param.12) | copy-start | bytes 52
  76.0 99.0 %all-to-all-start = ((f32[512,1,4,512]{0,3,1,2:T(8,128)}), f32[512,1,4,512]{0,3,1,2:T(8,128)}, u32[]{:S(2)}, u32[]{:S(2)}) async-start(f32[512,1,4,512]{0,3,1,2:T(8,128)} %bitcast.212), calls=%async_computation | async-start | bytes 8388608 | tf_op jit(solution)/shard_map/all_to_all | solution.py:139
  82.1 215.0 %reduce-scatter.2.cloned.1.call-start = ((), (), s32[]{:S(2)}) async-start(), calls=%async_computation.2 | async-start | bytes 5242880 | tf_op jit(solution)/shard_map/reduce_scatter | solution.py:154
  200.7 3.3 %copy-start.3 = (f32[1,256,2048]{1,0,2:T(1,128)S(1)}, f32[1,256,2048]{1,0,2:T(1,128)}, u32[]{:S(2)}) copy-start(f32[1,256,2048]{1,0,2:T(1,128)} %get-tuple-element.13) | copy-start | bytes 6291460
  208.1 1.3 copy-start
  209.5 3.8 %copy-start.2 = (f32[16,256,128]{2,0,1:T(8,128)S(1)}, f32[16,256,128]{2,0,1:T(8,128)}, u32[]{:S(2)}) copy-start(f32[16,256,128]{2,0,1:T(8,128)} %fusion.122) | copy-start | bytes 6291460
  238.8 3.1 %copy-start.1 = (f32[256,2048]{1,0:T(8,128)S(1)}, f32[256,2048]{1,0:T(8,128)}, u32[]{:S(2)}) copy-start(f32[256,2048]{1,0:T(8,128)} %copy.82) | copy-start | bytes 6291460
Sparse Core Ops, SparseCore 0:
  253.5 43.5 reduce-scatter.1
where the time goes:
time: 311 us; the launch traced here: 307 us
  waiting for transfers between devices  104 us (33%)
  matrix products  99.5 us (32%)
  local copies, waits for them, and re-layouts  58.1 us (19%)
  other arithmetic  19 us (6%)
  between operations  14 us (5%)
  starting transfers between devices  12.3 us (4%)
    all_to_all x1, waiting for transfers between devices, per_device(): lax.all_to_all(spectra, 'freq', split_axis=2, concat_axis=0, tiled=True)  69.5 us
    reduce_scatter x1, waiting for transfers between devices, per_device(): lax.psum_scatter(jnp.concatenate([term_real, term_imag], axis=1), ('read'...  34.6 us
    dot_general x2, matrix products, psf_spectrum(): jnp.einsum('ma,nap->nmp', sin_u, q_real, precision=HIGHEST)  11.6 us
    another operation x4, local copies, waits for them, and re-layouts  10.9 us
    dot_general x2, matrix products, fourier(): jnp.einsum('...db,bc->...cd', mid_re, sin_b, precision=HIGHEST)  10.1 us
    dot_general x2, matrix products, psf_spectrum(): jnp.einsum('ma,nap->nmp', sin_u, q_imag, precision=HIGHEST)  9.76 us
    dot_general x2, matrix products, fourier(): jnp.einsum('...db,bc->...cd', mid_im, cos_b, precision=HIGHEST)  9.33 us
    dot_general x2, matrix products, psf_spectrum(): jnp.einsum('ma,nap->nmp', cos_u, q_imag, precision=HIGHEST)  9.2 us
  transfers between devices with their start and end apart: 4, of which 2 were waited for; matrix products, arithmetic and copies ran while one was open for 14% of the time, Pallas kernels for 0%

commit v1 on v0

--- a/solution.py
+++ b/solution.py
@@ -7,6 +7,29 @@
 HIGHEST = lax.Precision.HIGHEST
 TWO_PI = 2.0 * math.pi
 LANES = 128
+
+
+def in_blocks(shard, dim, size):
+    dims = shard.shape
+    blocks = shard.reshape(*dims[:dim], size, dims[dim] // size, *dims[dim + 1 :])
+    return jnp.moveaxis(blocks, dim, 0)
+
+
+def laid_out(blocks, dim):
+    blocks = jnp.moveaxis(blocks, 0, dim)
+    dims = blocks.shape
+    return blocks.reshape(*dims[:dim], dims[dim] * dims[dim + 1], *dims[dim + 2 :])
+
+
+def swapped_with_each(array, axis, split_dim, concat_dim):
+    size, place = (lax.axis_size(axis), lax.axis_index(axis))
+    blocks = in_blocks(array, split_dim, size)
+    gathered = [blocks[place]]
+    for step in range(1, size):
+        sent = blocks[place ^ step]
+        gathered.append(lax.ppermute(sent, axis, [(i, i ^ step) for i in range(size)]))
+    blocks = jnp.stack(gathered)[place ^ jnp.arange(size)]
+    return laid_out(blocks, concat_dim)
 
 
 def with_halo(block, sides, width):
@@ -136,7 +159,7 @@
     spec_re, spec_im = fourier(cleaned, None, image_width)
     packed = pack_blocks(spec_re[:, :, :half_width], spec_im[:, :, :half_width], freq_count)
     spectra = jnp.transpose(packed, (1, 0, 2)).reshape(rows_dev, exp_dev, freq_count, 2 * per_freq)
-    regrouped = lax.all_to_all(spectra, "freq", split_axis=2, concat_axis=0, tiled=True)
+    regrouped = swapped_with_each(spectra, "freq", 2, 0)
     regrouped = regrouped.reshape(image_height, exp_dev, 2, per_freq)
     col_re = jnp.transpose(regrouped[:, :, 0], (1, 2, 0))
     col_im = jnp.transpose(regrouped[:, :, 1], (1, 2, 0))

time: 311 us -> 317 us (1.019)
  local copies, waits for them, and re-layouts: 58.1 us -> 65.9 us
  other arithmetic: 19 us -> 23.4 us
  waiting for transfers between devices: 104 us -> 99.8 us
    all_to_all x1 -> x0, waiting for transfers between devices: 69.5 us -> none  [per_device(): lax.all_to_all(spectra, 'freq', split_axis=2, concat_axis=0, tiled=True)]
    ppermute x0 -> x3, waiting for transfers between devices: none -> 48.2 us  [swapped_with_each(): lax.ppermute(sent, axis, [(i, i ^ step) for i in range(size)])]
    reduce_scatter x1, waiting for transfers between devices: 34.6 us -> 51.6 us  [per_device(): lax.psum_scatter(jnp.concatenate([term_real, term_imag], axis=1), ('read'...]
    unnamed x23 -> x21, local copies, waits for them, and re-layouts: 5.2 us -> 14.3 us
    slice x0 -> x1, local copies, waits for them, and re-layouts: none -> 8.06 us  [per_device(): col_im = jnp.transpose(regrouped[:, :, 1], (1, 2, 0))]
    transpose x1 -> x0, local copies, waits for them, and re-layouts: 7.57 us -> none  [per_device(): col_im = jnp.transpose(regrouped[:, :, 1], (1, 2, 0))]
    all_to_all x1 -> x0, starting transfers between devices: 6.1 us -> none  [per_device(): lax.all_to_all(spectra, 'freq', split_axis=2, concat_axis=0, tiled=True)]
    reshape x1 -> x0, local copies, waits for them, and re-layouts: 5.88 us -> none  [per_device(): regrouped = regrouped.reshape(image_height, exp_dev, 2, per_freq)]
  transfers between devices with their start and end apart: 4 -> 6, of which waited for: 2 -> 3; matrix products, arithmetic and copies ran while one was open for 14% -> 16% of each run, Pallas kernels for 0% -> 0%
where the time goes in v1:
time: 317 us; the launch traced here: 313 us
  waiting for transfers between devices  99.8 us (31%)
  matrix products  98.6 us (31%)
  local copies, waits for them, and re-layouts  65.9 us (21%)
  other arithmetic  23.4 us (7%)
  between operations  14.1 us (4%)
  starting transfers between devices  11.5 us (4%)
    reduce_scatter x1, waiting for transfers between devices, per_device(): lax.psum_scatter(jnp.concatenate([term_real, term_imag], axis=1), ('read'...  51.6 us
    ppermute x3, waiting for transfers between devices, swapped_with_each(): lax.ppermute(sent, axis, [(i, i ^ step) for i in range(size)])  48.2 us
    unnamed x21, local copies, waits for them, and re-layouts  14.3 us
    dot_general x2, matrix products, psf_spectrum(): jnp.einsum('ma,nap->nmp', sin_u, q_real, precision=HIGHEST)  12.7 us
    another operation x7, local copies, waits for them, and re-layouts  12.1 us
    dot_general x2, matrix products, psf_spectrum(): jnp.einsum('ma,nap->nmp', sin_u, q_imag, precision=HIGHEST)  10.8 us
    dot_general x2, matrix products, fourier(): jnp.einsum('...db,bc->...cd', mid_re, sin_b, precision=HIGHEST)  10.1 us
    dot_general x2, matrix products, psf_spectrum(): jnp.einsum('ma,nap->nmp', cos_u, q_imag, precision=HIGHEST)  9.86 us
  transfers between devices with their start and end apart: 6, of which 3 were waited for; matrix products, arithmetic and copies ran while one was open for 16% of the time, Pallas kernels for 0%

profile of v1, /device:TPU:0, one launch (start us, length us, event | category | flops | bytes accessed | tf_op | source)
XLA Modules:
  0.0 313.3 jit_solution(13764863678785626536)
XLA Ops:
  7.4 4.9 %collective-permute-start = (f32[1,1,2048]{2,1,0:T(1,128)S(1)}, f32[1,1,2048]{2,1,0:T(1,128)S(1)}, u32[]{:S(2)}, u32[]{:S(2)}) collective-permute-start(f32[1,1,2048]{2,1,0:T(1,128)S(1)} %get-tuple-element.21), channel_id=1, source_target_pairs={{0,4},{4,8},{8,12},{1,5},{5,9},{9,13},{2,6},{6,10},{10,14},{3,7},{... | collective-permute-start | bytes 24584 | tf_op jit(solution)/shard_map/ppermute | solution.py:40
  13.7 8.0 %fusion.262 = (f32[1,512,2047]{2,1,0:T(8,128)}, f32[1,512,2047]{2,1,0:T(8,128)}) fusion(f32[1,512,2048]{2,1,0:T(8,128)} %param.7), kind=kLoop, calls=%fused_computation.303 | loop fusion | bytes 16769024 | tf_op jit(solution)/shard_map/slice | solution.py:147
  23.8 1.3 fusion.178
  27.8 9.1 %fusion.6 = f32[64,8,16,128]{3,1,2,0:T(8,128)S(1)} fusion(f32[1,512,2048]{2,1,0:T(8,128)} %param.7, f32[1,1,2048]{2,1,0:T(1,128)S(1)} %collective-permute-done.1, f32[1,1,2048]{2,1,0:T(1,128)S(1)} %collective-permute-done, f32[1,512,2047]{2,1,0:T(8,128)} %get-tuple-element.20, f32[1,512,2047]{2,1,0:T(8,128)} %get-tuple-element.19, pred[512]{0:T(512)(128)(4,1)S(1)} %fusion.151), kind=kLoop, calls=%fused_computation.8 | loop fusion | flops 8388608 | bytes 16790016
  37.9 4.0 %fusion.119 = f32[16,512,128]{2,0,1:T(8,128)S(1)} fusion(f32[512,16,128]{2,1,0:T(8,128)S(1)} %bitcast.218), kind=kOutput, calls=%fused_computation.151 | convolution fusion | flops 201330176 | bytes 8388608 | tf_op jit(solution)/shard_map/...ab,ad->...db/dot_general | solution.py:63
  41.9 4.8 %fusion.8 = (f32[512,16,128]{2,1,0:T(8,128)S(1)}, f32[512,16,128]{2,1,0:T(8,128)S(1)}) fusion(f32[16,512,128]{2,0,1:T(8,128)S(1)} %fusion.119, f32[16,128]{1,0:T(8,128)S(1)} %get-tuple-element.27, f32[16,128]{1,0:T(8,128)S(1)} %get-tuple-element.28, f32[512,16,128]{2,1,0:T(8,128)S(1)} %bitcast.219), kind=kOutput, calls=%fused_computation.16 | convolution fusion | flops 208670208 | bytes 16793600 | tf_op jit(solution)/shard_map/...ab,ad->...db/dot_general | solution.py:62
  46.8 5.9 %fusion.13 = f32[128,512,16]{1,0,2:T(8,128)S(1)} fusion(f32[512,16,128]{2,1,0:T(8,128)S(1)} %get-tuple-element.8), kind=kOutput, calls=%fused_computation.25 | convolution fusion | flops 1610842112 | bytes 8388608 | tf_op jit(solution)/shard_map/...db,bc->...cd/dot_general | solution.py:76
  52.7 5.4 %fusion.11 = f32[128,512,16]{1,0,2:T(8,128)S(1)} fusion(f32[512,16,128]{2,1,0:T(8,128)S(1)} %get-tuple-element.8), kind=kOutput, calls=%fused_computation.23 | convolution fusion | flops 1610842112 | bytes 8388608 | tf_op jit(solution)/shard_map/...db,bc->...cd/dot_general | solution.py:79
  58.1 6.2 %add_bitcast_fusion = f32[1,512,128,16]{1,2,3,0:T(8,128)S(1)} fusion(f32[128,512,16]{1,0,2:T(8,128)S(1)} %fusion.13, f32[512,16,128]{2,1,0:T(8,128)S(1)} %get-tuple-element.7), kind=kOutput, calls=%fused_computation.22 | convolution fusion | flops 1611890688 | bytes 12582912 | tf_op jit(solution)/shard_map/...db,bc->...cd/dot_general | solution.py:76
  64.3 2.4 copy.20
  66.9 5.9 %subtract_bitcast_fusion = f32[1,512,128,16]{1,2,3,0:T(8,128)S(1)} fusion(f32[128,512,16]{1,0,2:T(8,128)S(1)} %fusion.11, f32[512,16,128]{2,1,0:T(8,128)S(1)} %get-tuple-element.7), kind=kOutput, calls=%fused_computation.21 | convolution fusion | flops 1611890688 | bytes 12582912 | tf_op jit(solution)/shard_map/...db,bc->...cd/dot_general | solution.py:79
  72.8 2.6 copy.23
  76.1 1.5 constant_dynamic-slice_fusion.3
  77.6 2.6 copy.27
  80.2 2.6 collective-permute-start.2
  84.2 2.6 collective-permute-start.3
  87.2 5.7 %fusion.61 = f32[256,2048]{1,0:T(8,128)S(1)} fusion(f32[16,256]{1,0:T(8,128)S(1)} %fusion.129, s32[16]{0:T(128)S(1)} %and_select_fusion), kind=kOutput, calls=%fused_computation.88 | convolution fusion | flops 101122048 | bytes 2113600 | tf_op jit(solution)/shard_map/ma,nap->nmp/dot_general | solution.py:114
  92.8 7.0 %fusion.59 = f32[256,2048]{1,0:T(8,128)} fusion(f32[16,256]{1,0:T(8,128)S(1)} %convolution_negate_fusion.1, s32[16]{0:T(128)S(1)} %and_select_fusion), kind=kOutput, calls=%fused_computation.87 | convolution fusion | flops 101122048 | bytes 2113600 | tf_op jit(solution)/shard_map/ma,nap->nmp/dot_general | solution.py:117
  99.9 8.0 %fusion.22 = f32[2048,256]{0,1:T(8,128)} fusion(f32[256,2048]{1,0:T(8,128)S(1)} %fusion.61, f32[16,256]{1,0:T(8,128)S(1)} %convolution_negate_fusion.1, f32[]{:T(128)} %get-tuple-element.26, s32[16]{0:T(128)S(1)} %and_select_fusion), kind=kOutput, calls=%fused_computation.36 | convolution fusion | flops 102170624 | bytes 4210756 | tf_op jit(solution)/shard_map/ma,nap->nmp/dot_general | solution.py:114
  108.2 18.3 %collective-permute-done.2 = f32[512,1,1,512]{3,0,2,1:T(8,128)} collective-permute-done((f32[512,1,1,512]{3,0,2,1:T(8,128)}, f32[512,1,1,512]{3,0,2,1:T(8,128)}, u32[]{:S(2)}, u32[]{:S(2)}) %collective-permute-start.2) | collective-permute-done | bytes 1048608 | tf_op jit(solution)/shard_map/ppermute | solution.py:30
  126.5 29.9 %collective-permute-done.3 = f32[512,1,1,512]{3,0,2,1:T(8,128)} collective-permute-done((f32[512,1,1,512]{3,0,2,1:T(8,128)}, f32[512,1,1,512]{3,0,2,1:T(8,128)}, u32[]{:S(2)}, u32[]{:S(2)}) %collective-permute-start.3) | collective-permute-done | bytes 1048608 | tf_op jit(solution)/shard_map/ppermute | solution.py:30
  156.4 4.3 %maximum_bitcast_fusion = f32[4,512,512]{2,1,0:T(8,128)} fusion(f32[1,512,1,1,512]{4,1,0,3,2:T(8,128)} %bitcast.31, f32[1,512,1,1,512]{4,1,0,3,2:T(8,128)} %bitcast.29, f32[1,512,1,1,512]{4,1,0,3,2:T(8,128)} %bitcast.27, f32[1,512,1,1,512]{4,1,0,3,2:T(8,128)S(1)} %bitcast.233), kind=kLoop, calls=%fused_computation.11 | loop fusion | flops 3145728 | bytes 8388608 | tf_op jit(solution)/shard_map/stack | solution.py:31
  160.8 5.0 %gather_fusion = f32[4,512,512]{2,1,0:T(8,128)} fusion(f32[4,512,512]{2,1,0:T(8,128)} %maximum_bitcast_fusion, s32[1024]{0:T(1024)S(1)} %pad_clamp_fusion), kind=kCustom, calls=%fused_computation | custom fusion | bytes 8388624 | tf_op jit(solution)/shard_map/gather | solution.py:31
  165.7 5.9 %reshape_reshape.3 = f32[2048,1,2,256]{3,2,0,1:T(2,128)} reshape(f32[4,512,512]{2,1,0:T(8,128)} %gather_fusion) | data formatting | bytes 8388608 | tf_op jit(solution)/shard_map/reshape;reshape | solution.py:163
  171.6 8.1 %fusion.261 = (f32[2048,1,1,256]{3,2,0,1:T(1,128)}, f32[2048,1,1,256]{3,2,0,1:T(1,128)}) fusion(f32[2048,1,2,256]{3,2,0,1:T(2,128)} %reshape_reshape.3), kind=kLoop, calls=%fused_computation.302 | loop fusion | bytes 8388608 | tf_op jit(solution)/shard_map/slice | solution.py:165
  179.7 4.6 %copy.44 = f32[2048,1,1,256]{0,3,2,1:T(8,128)S(1)} copy(f32[2048,1,1,256]{3,2,0,1:T(1,128)} %get-tuple-element.14) | data formatting | bytes 4194304
  184.6 1.9 fusion.116
  186.6 3.3 %fusion.122 = f32[16,256,128]{2,0,1:T(8,128)} fusion(f32[256,16,128]{2,1,0:T(8,128)S(1)} %bitcast.223), kind=kOutput, calls=%fused_computation.154 | convolution fusion | flops 100666880 | bytes 4194304 | tf_op jit(solution)/shard_map/...ab,ad->...db/dot_general | solution.py:62
  189.9 6.4 %copy.45 = f32[2048,1,1,256]{0,3,2,1:T(8,128)} copy(f32[2048,1,1,256]{3,2,0,1:T(1,128)} %get-tuple-element.13) | data formatting | bytes 4194304
  196.3 2.0 copy.48
  198.3 2.1 negate_add_fusion
  200.4 2.5 fusion.31
  202.8 2.6 fusion.36
  205.4 3.9 %fusion.34 = f32[128,256,16]{1,0,2:T(8,128)} fusion(f32[256,16,128]{2,1,0:T(8,128)S(1)} %get-tuple-element.12), kind=kOutput, calls=%fused_computation.56 | convolution fusion | flops 805535744 | bytes 4194304 | tf_op jit(solution)/shard_map/...db,bc->...cd/dot_general | solution.py:79
  209.3 2.8 add_bitcast_fusion.1
  212.1 2.5 copy.34
  214.7 2.9 copy.35
  217.6 4.2 %subtract_bitcast_fusion.1 = f32[1,256,128,16]{1,2,3,0:T(8,128)S(1)} fusion(f32[128,256,16]{1,0,2:T(8,128)} %fusion.34, f32[256,16,128]{2,1,0:T(8,128)S(1)} %get-tuple-element.11), kind=kOutput, calls=%fused_computation.53 | convolution fusion | flops 806060032 | bytes 6291456 | tf_op jit(solution)/shard_map/...db,bc->...cd/dot_general | solution.py:79
  221.8 2.5 copy.38
  224.4 3.1 copy.39
  227.5 9.1 %fusion.28 = (f32[2048,256]{0,1:T(8,128)S(1)}, f32[2048,256]{0,1:T(8,128)S(1)}) fusion(f32[256,2048]{1,0:T(8,128)} %copy.39, f32[2048,256]{0,1:T(8,128)} %fusion.22, f32[256,2048]{1,0:T(8,128)S(1)} %copy-done, f32[256,2048]{1,0:T(8,128)} %fusion.59, f32[16,256]{1,0:T(8,128)S(1)} %fusion.129, s32[16]{0:T(128)S(1)} %and_select_fusion, f32[]{:T(128)} %get-tuple-element.26), kind=kOutput, calls=%fused_computation.41 | convolution fusion | flops 105316352 | bytes 12599364 | tf_op jit(solution)/shard_map/ma,nap->nmp/dot_general | solution.py:117
  236.5 2.4 pad_maximum_fusion.3
  239.7 2.8 fusion.69
  242.5 2.8 fusion.71
  245.4 2.8 fusion.73
  248.2 3.6 %fusion.27 = f32[512,256]{0,1:T(8,128)S(1)} fusion(f32[4,256,512]{2,1,0:T(8,128)S(1)} %fusion.71, f32[4,256,512]{2,1,0:T(8,128)S(1)} %fusion.73, f32[4,256,512]{2,1,0:T(8,128)S(1)} %fusion.69, f32[4,16,256]{2,1,0:T(8,128)S(1)} %convolution_bitcast_fusion, f32[4]{0:T(128)S(1)} %get-tuple-element.25, s32[16]{0:T(128)S(1)} %and_select_fusion, ...), kind=kOutput, calls=%fused_computation.38 | convolution fusion | flops 104316928 | bytes 6883408 | tf_op jit(solution)/shard_map/ma,nap->nmp/dot_general | solution.py:117
  251.8 51.6 %reduce-scatter.2.cloned.1.call-done = f32[512,512]{0,1:T(8,128)} async-done(((f32[2048,512]{0,1:T(8,128)}), f32[512,512]{0,1:T(8,128)}) %reduce-scatter.2.cloned.1.call-update) | async-done | bytes 1048592 | tf_op jit(solution)/shard_map/reduce_scatter | solution.py:177
  303.4 1.4 fusion.56
  (49 shorter events, 13.1 us)
Async XLA Ops:
  6.5 296.9 %reduce-scatter.2.cloned.1.call-start = ((), (), s32[]{:S(2)}) async-start(), calls=%async_computation.1 | async-start | bytes 5242880 | tf_op jit(solution)/shard_map/reduce_scatter | solution.py:177
  7.4 20.4 %collective-permute-start = (f32[1,1,2048]{2,1,0:T(1,128)S(1)}, f32[1,1,2048]{2,1,0:T(1,128)S(1)}, u32[]{:S(2)}, u32[]{:S(2)}) collective-permute-start(f32[1,1,2048]{2,1,0:T(1,128)S(1)} %get-tuple-element.21), channel_id=1, source_target_pairs={{0,4},{4,8},{8,12},{1,5},{5,9},{9,13},{2,6},{6,10},{10,14},{3,7},{... | collective-permute-start | bytes 24584 | tf_op jit(solution)/shard_map/ppermute | solution.py:40
  12.4 15.5 %collective-permute-start.1 = (f32[1,1,2048]{2,1,0:T(1,128)S(1)}, f32[1,1,2048]{2,1,0:T(1,128)S(1)}, u32[]{:S(2)}, u32[]{:S(2)}) collective-permute-start(f32[1,1,2048]{2,1,0:T(1,128)S(1)} %get-tuple-element.22), channel_id=1, source_target_pairs={{4,0},{8,4},{12,8},{5,1},{9,5},{13,9},{6,2},{10,6},{14,10},{7,3},{... | collective-permute-start | bytes 24584 | tf_op jit(solution)/shard_map/ppermute | solution.py:43
  13.7 8.2 %copy-start.7 = (s32[4]{0:T(128)S(1)}, s32[4]{0:T(128)}, u32[]{:S(2)}) copy-start(s32[4]{0:T(128)} %param.13) | copy-start | bytes 52
  13.7 9.4 %copy-start.2 = (f32[4,16,16]{2,1,0:T(8,128)S(1)}, f32[4,16,16]{2,1,0:T(8,128)}, u32[]{:S(2)}) copy-start(f32[4,16,16]{2,1,0:T(8,128)} %param.8) | copy-start | bytes 12292
  13.7 10.1 %copy-start.3 = (s32[4,2]{0,1:T(2,128)S(1)}, s32[4,2]{0,1:T(2,128)}, u32[]{:S(2)}) copy-start(s32[4,2]{0,1:T(2,128)} %param.11) | copy-start | bytes 100
  13.7 11.4 %copy-start.4 = (f32[4]{0:T(128)S(1)}, f32[4]{0:T(128)}, u32[]{:S(2)}) copy-start(f32[4]{0:T(128)} %param.10) | copy-start | bytes 52
  13.7 11.4 %copy-start.5 = (f32[4]{0:T(128)S(1)}, f32[4]{0:T(128)}, u32[]{:S(2)}) copy-start(f32[4]{0:T(128)} %param.9) | copy-start | bytes 52
  13.7 11.4 %copy-start.6 = (s32[4]{0:T(128)S(1)}, s32[4]{0:T(128)}, u32[]{:S(2)}) copy-start(s32[4]{0:T(128)} %param.12) | copy-start | bytes 52
  80.2 46.3 %collective-permute-start.2 = (f32[512,1,1,512]{3,0,2,1:T(8,128)}, f32[512,1,1,512]{3,0,2,1:T(8,128)}, u32[]{:S(2)}, u32[]{:S(2)}) collective-permute-start(f32[512,1,1,512]{3,0,2,1:T(8,128)} %bitcast.234), channel_id=1, source_target_pairs={{0,4},{4,0},{8,12},{12,8},{1,5},{5,1},{9,13},{13,9},{2,6},{6,2},{1... | collective-permute-start | bytes 3145736 | tf_op jit(solution)/shard_map/ppermute | solution.py:30
  84.2 72.3 %collective-permute-start.3 = (f32[512,1,1,512]{3,0,2,1:T(8,128)}, f32[512,1,1,512]{3,0,2,1:T(8,128)}, u32[]{:S(2)}, u32[]{:S(2)}) collective-permute-start(f32[512,1,1,512]{3,0,2,1:T(8,128)} %bitcast.235), channel_id=1, source_target_pairs={{0,8},{4,12},{8,0},{12,4},{1,9},{5,13},{9,1},{13,5},{2,10},{6,14},... | collective-permute-start | bytes 3145736 | tf_op jit(solution)/shard_map/ppermute | solution.py:30
  87.1 69.3 %collective-permute-start.4 = (f32[512,1,1,512]{3,0,2,1:T(8,128)S(1)}, f32[512,1,1,512]{3,0,2,1:T(8,128)}, u32[]{:S(2)}, u32[]{:S(2)}) collective-permute-start(f32[512,1,1,512]{3,0,2,1:T(8,128)S(1)} %bitcast.236), channel_id=1, source_target_pairs={{0,12},{4,8},{8,4},{12,0},{1,13},{5,9},{9,5},{13,1},{2,14},{6,10},... | collective-permute-start | bytes 3145736 | tf_op jit(solution)/shard_map/ppermute | solution.py:30
  198.3 2.1 copy-start.1
  224.4 3.1 copy-start
Sparse Core Ops, SparseCore 0:
  239.1 64.2 reduce-scatter.1
